TPU v7x, 512 devices: a whole 4x4x16 slice. The times are simulated.
512 devices in a mesh: dp: 64 (over y_hi, z, core), tensor: 8 (over x, y_lo).
Axes of the slice: x: 4, y: 4 (y_hi: 2, y_lo: 2; y = y_hi * 2 + y_lo), z: 16, core: 2. Of those that a mesh axis runs over, the one named last changes fastest.
Arguments:
- inputs: bfloat16 [16384, 2560], P('dp', 'tensor'), may hold values from -37 to 37
- gate_values: bfloat16 [16384, 8192], P('dp', 'tensor'), may hold values from -8 to 8
- up_values: bfloat16 [16384, 8192], P('dp', 'tensor'), may hold values from -6 to 6
- hidden_cotangent: bfloat16 [16384, 8192], P('dp', 'tensor'), may hold values from -37 to 37
- owners: int32 [8, 16], P('tensor'), may hold values from 0 to 15, each once within a row
- left_inverse: float32 [64, 8, 320, 320], P('dp', 'tensor'), may hold values from -2 to 16, as said below
- right_inverse: float32 [64, 8, 512, 128], P('dp', 'tensor'), may hold values from -2 to 16, as said below
Outputs:
- input_factor: float32 [8, 320, 320], P('tensor', 'dp')
- output_factor: float32 [8, 1024, 512], P('tensor', 'dp')
- preconditioned: float32 [8, 320, 8192], P(None, 'dp', 'tensor')
Inputs may be any that keep to these rules, and one draw needn't show every extreme that they name: `owners`: each row is an ordering of the 16 worker groups. `left_inverse`: diagonal entries lie in 4 to 16. `right_inverse`: block [i, t] is columns (i % 4) * 128 onward of a matrix whose diagonal entries lie in 4 to 16.
All inputs are finite; a program needn't handle non-finite values.
Results may differ from a plain program's by a relative error of at most 0.0029.
Values may be sent and summed in bfloat16 or wider, within the bound.
A program may use at most 128 MiB of HBM per device.

v0:
```python
import jax
import jax.numpy as jnp
from jax import lax
from jax.sharding import PartitionSpec as P

HIGHEST = lax.Precision.HIGHEST


def swapped(value, axis, bit):
    mask = 2**bit
    pairs = [(source, source ^ mask) for source in range(lax.axis_size(axis))]
    return lax.ppermute(value, axis, pairs)


def gate_gradient(gate_values, up_values, hidden_cotangent):
    pre_act = gate_values.astype(jnp.float32)
    sigma = jax.nn.sigmoid(pre_act)
    slope = sigma * (1.0 + pre_act * (1.0 - sigma))
    return (hidden_cotangent.astype(jnp.float32) * up_values.astype(jnp.float32) * slope).astype(
        jnp.bfloat16
    )


def factor_sums(input_part, output_part):
    return (
        lax.psum_scatter(input_part, "dp", scatter_dimension=0, tiled=True),
        lax.psum_scatter(output_part, "dp", scatter_dimension=0, tiled=True),
    )


def add_rows(received):
    return jnp.sum(received, axis=0)


def shards(inputs, gate_values, up_values, hidden_cotangent, owners, left_inverse, right_inverse):
    data_size = lax.axis_size("dp")
    group_size = lax.axis_size("tensor")
    token_rows = inputs.shape[0]
    block_in = inputs.shape[1]
    hid_local = gate_values.shape[1]
    block_out = right_inverse.shape[2]
    col_piece = right_inverse.shape[3]
    workers = block_out // col_piece
    tile_count = data_size // workers
    col_blocks = hid_local // block_out
    total = token_rows * data_size
    row_share = block_in // data_size
    row_piece = block_in // workers
    worker_bits = workers.bit_length() - 1
    device_rank = lax.axis_index("dp")
    gate_grad = gate_gradient(gate_values, up_values, hidden_cotangent)
    product = lax.dot_general(
        lax.all_gather(inputs, "tensor", axis=1, tiled=True),
        gate_grad,
        (((0,), (0,)), ((), ())),
        preferred_element_type=jnp.float32,
    )
    weight_grad = product / total
    input_part = (
        lax.dot_general(
            inputs, inputs, (((0,), (0,)), ((), ())), preferred_element_type=jnp.float32
        )
        / total
    )
    split_grad = gate_grad.reshape(token_rows, col_blocks, block_out)
    output_part = (
        jnp.einsum("tci,tcj->cij", split_grad, split_grad, preferred_element_type=jnp.float32)
        / total
    )
    output_part = output_part.reshape(hid_local, block_out)
    tiles = weight_grad.reshape(group_size, block_in, col_blocks, block_out).transpose(0, 2, 1, 3)
    tiles = tiles.reshape(tile_count, block_in, block_out)
    owner_row = owners[0]
    holders = jnp.argsort(owner_row)
    outgoing = jnp.take(tiles, holders, axis=0)
    pieces = outgoing.reshape(data_size, row_piece, block_out)
    own_piece = add_rows(lax.all_to_all(pieces, "dp", split_axis=0, concat_axis=0, tiled=True))
    input_share, output_share = factor_sums(input_part, output_part)
    full_tile = own_piece
    for section_bit in range(worker_bits):
        other_piece = swapped(full_tile, "dp", section_bit)
        lower_side = device_rank >> section_bit & 1 == 0
        full_tile = jnp.where(
            lower_side,
            jnp.concatenate([full_tile, other_piece], 0),
            jnp.concatenate([other_piece, full_tile], 0),
        )
    right_part = jnp.dot(
        full_tile, right_inverse[0, 0], precision=HIGHEST, preferred_element_type=jnp.float32
    )
    finished = jnp.dot(
        left_inverse[0, 0], right_part, precision=HIGHEST, preferred_element_type=jnp.float32
    )
    returned = lax.all_to_all(
        finished.reshape(data_size, row_share, col_piece),
        "dp",
        split_axis=0,
        concat_axis=0,
        tiled=True,
    )
    by_group = returned.reshape(tile_count, workers, row_share, col_piece)
    ordered = jnp.take(by_group, owner_row, axis=0)
    placed = ordered.reshape(group_size, col_blocks, workers, row_share, col_piece).transpose(
        0, 3, 1, 2, 4
    )
    preconditioned = placed.reshape(group_size, row_share, hid_local)
    return (input_share[None], output_share[None], preconditioned)


def solution(mesh):
    in_specs = (
        P("dp", "tensor"),
        P("dp", "tensor"),
        P("dp", "tensor"),
        P("dp", "tensor"),
        P("tensor", None),
        P("dp", "tensor", None, None),
        P("dp", "tensor", None, None),
    )
    out_specs = (P("tensor", "dp", None), P("tensor", "dp", None), P(None, "dp", "tensor"))
    return jax.shard_map(shards, mesh=mesh, in_specs=in_specs, out_specs=out_specs, check_vma=False)
```

profile of v0, /device:TPU:1, one launch (start us, length us, event | category | flops | bytes accessed | tf_op | source)
XLA Modules:
  0.0 979.7 jit_solution(18159188199430180696)
XLA Ops:
  8.1 0.7 all-gather.2.cloned.1.call-update
  8.8 1.9 sort.17
  10.9 1.9 fusion.6
  12.7 48.5 %all-gather.2.cloned.1.call-done = bf16[256,2560]{0,1:T(8,128)(2,1)} async-done(((bf16[256,320]{0,1:T(8,128)(2,1)}), bf16[256,2560]{0,1:T(8,128)(2,1)}) %all-gather.2.cloned.1.call-update) | async-done | bytes 1310736 | tf_op jit(solution)/shard_map/all_gather | solution.py:53
  61.3 6.8 multiply_bitcast_fusion
  68.1 13.6 %reshape.97 = f32[8,320,2,512]{1,0,3,2:T(8,128)} reshape(f32[2560,1024]{0,1:T(8,128)} %multiply_bitcast_fusion) | data formatting | bytes 20971520 | tf_op jit(solution)/shard_map/reshape | solution.py:71
  81.6 14.4 %copy.44 = f32[8,320,2,512]{3,2,1,0:T(2,128)} copy(f32[8,320,2,512]{1,0,3,2:T(8,128)} %reshape.97) | data formatting | bytes 20971520 | tf_op jit(solution)/shard_map/reshape | solution.py:71
  96.1 9.9 %copy.38 = f32[8,2,320,512]{3,2,1,0:T(8,128)} copy(f32[8,2,320,512]{3,1,2,0:T(2,128)} %bitcast.41) | data formatting | bytes 20971520 | tf_op jit(solution)/shard_map/transpose | solution.py:71
  106.0 9.0 gather_fusion
  115.0 10.3 %broadcast_select_fusion = f32[64,80,512]{2,1,0:T(8,128)} fusion(f32[64,80,512]{2,1,0:T(8,128)} %bitcast.39, pred[64]{0:T(512)(128)(4,1)S(1)} %broadcast_in_dim.36), kind=kLoop, calls=%fused_computation.3 | loop fusion | flops 2621440 | bytes 20971584 | tf_op jit(solution)/shard_map/jit(_take)/select_n | solution.py:75
  125.4 19.8 %all-to-all-start = ((f32[64,80,512]{2,1,0:T(8,128)}), f32[64,80,512]{2,1,0:T(8,128)}, u32[]{:S(2)}, u32[]{:S(2)}) async-start(f32[64,80,512]{2,1,0:T(8,128)} %broadcast_select_fusion), calls=%async_computation.1 | async-start | bytes 20971520 | tf_op jit(solution)/shard_map/all_to_all | solution.py:77
  145.3 1.1 convolution_multiply_fusion.1
  146.4 1.8 convolution_multiply_fusion
  148.3 455.7 %all-to-all-done = f32[64,80,512]{2,1,0:T(8,128)} async-done(((f32[64,80,512]{2,1,0:T(8,128)}), f32[64,80,512]{2,1,0:T(8,128)}, u32[]{:S(2)}, u32[]{:S(2)}) %all-to-all-start) | async-done | bytes 10485792 | tf_op jit(solution)/shard_map/all_to_all | solution.py:77
  604.0 4.9 reduce_sum.9
  608.9 2.3 collective-permute-start
  611.2 1.0 collective-permute-done
  612.3 5.9 collective-permute-start.1
  618.2 0.5 broadcast.73
  618.7 0.7 reduce.3
  619.5 1.3 dynamic-slice
  621.4 4.5 collective-permute-done.1
  625.9 0.7 fusion.7
  626.6 0.5 convolution_bitcast_fusion
  627.2 0.7 reshape.77
  627.9 9.1 all-to-all-start.1
  637.0 132.9 %all-reduce.3.cloned.1.call-done = f32[320,320]{1,0:T(8,128)} async-done(((f32[320,320]{1,0:T(8,128)}), f32[320,320]{1,0:T(8,128)}) %all-reduce.3.cloned.1.call-update) | async-done | bytes 409616
  769.9 0.7 dynamic-slice_bitcast_fusion
  770.7 0.6 copy.43
  771.3 0.6 gather_fusion.1
  772.1 0.7 copy.42
  772.8 199.5 %reduce-scatter.2.cloned.1.call-done = f32[16,512]{1,0:T(8,128)} async-done(((f32[1024,512]{1,0:T(8,128)}), f32[16,512]{1,0:T(8,128)}) %reduce-scatter.2.cloned.1.call-update) | async-done | bytes 32784 | tf_op jit(solution)/shard_map/reduce_scatter | solution.py:27
  (28 shorter events, 0.7 us)
Async XLA Ops:
  8.0 618.6 %copy-start = (f32[1,1,320,320]{3,2,1,0:T(8,128)S(1)}, f32[1,1,320,320]{3,2,1,0:T(8,128)}, u32[]{:S(2)}) copy-start(f32[1,1,320,320]{3,2,1,0:T(8,128)} %param.12) | copy-start | bytes 1228804
  8.0 53.3 %all-gather.2.cloned.1.call-start = ((), (), s32[]{:S(2)}) async-start(), calls=%async_computation.4 | async-start | bytes 1474560 | tf_op jit(solution)/shard_map/all_gather | solution.py:53
  125.4 19.9 %copy-start.1 = (bf16[256,320]{0,1:T(8,128)(2,1)S(1)}, bf16[256,320]{0,1:T(8,128)(2,1)}, u32[]{:S(2)}) copy-start(bf16[256,320]{0,1:T(8,128)(2,1)} %param.7) | copy-start | bytes 491524
  125.4 478.6 %all-to-all-start = ((f32[64,80,512]{2,1,0:T(8,128)}), f32[64,80,512]{2,1,0:T(8,128)}, u32[]{:S(2)}, u32[]{:S(2)}) async-start(f32[64,80,512]{2,1,0:T(8,128)} %broadcast_select_fusion), calls=%async_computation.1 | async-start | bytes 20971520 | tf_op jit(solution)/shard_map/all_to_all | solution.py:77
  145.2 473.6 %copy-start.3 = (s32[1,16]{1,0:T(1,128)S(1)}, s32[1,16]{1,0:T(1,128)}, u32[]{:S(2)}) copy-start(s32[1,16]{1,0:T(1,128)} %param.11) | copy-start | bytes 196
  145.2 480.7 %copy-start.2 = (f32[1,1,512,128]{3,2,1,0:T(8,128)S(1)}, f32[1,1,512,128]{3,2,1,0:T(8,128)}, u32[]{:S(2)}) copy-start(f32[1,1,512,128]{3,2,1,0:T(8,128)} %param.13) | copy-start | bytes 786436
  145.2 624.7 %all-reduce.3.cloned.1.call-start = ((), (), s32[]{:S(2)}) async-start(), calls=%async_computation.5 | async-start | bytes 983040
  146.4 825.9 %reduce-scatter.2.cloned.1.call-start = ((), (), s32[]{:S(2)}) async-start(), calls=%async_computation.3 | async-start | bytes 2129920 | tf_op jit(solution)/shard_map/reduce_scatter | solution.py:27
  608.9 3.3 collective-permute-start
  612.3 13.7 %collective-permute-start.1 = (f32[160,512]{1,0:T(8,128)S(1)}, f32[160,512]{1,0:T(8,128)S(1)}, u32[]{:S(2)}, u32[]{:S(2)}) collective-permute-start(f32[160,512]{1,0:T(8,128)S(1)} %maximum_select_fusion.2), channel_id=1, source_target_pairs={{0,16},{8,24},{16,0},{24,8},{32,48},{40,56},{48,32},{56,40},{64,80... | collective-permute-start | bytes 983048 | tf_op jit(solution)/shard_map/ppermute | solution.py:12
  627.9 143.4 %all-to-all-start.1 = ((f32[64,5,128]{2,1,0:T(8,128)}), f32[64,5,128]{2,1,0:T(8,128)S(1)}, u32[]{:S(2)}, u32[]{:S(2)}) async-start(f32[64,5,128]{2,1,0:T(8,128)} %reshape.77), calls=%async_computation.2 | async-start | bytes 524288 | tf_op jit(solution)/shard_map/all_to_all | solution.py:94
Sparse Core Ops, SparseCore 0:
  10.9 50.2 all-gather.1
Sparse Core Ops, SparseCore 1:
  148.6 621.3 all-reduce.2
  775.7 196.5 reduce-scatter.1
where the time goes:
time: 992 us; the launch traced here: 980 us
  waiting for transfers between devices  843 us (85%)
  local copies, waits for them, and re-layouts  52.5 us (5%)
  starting transfers between devices  37.3 us (4%)
  other arithmetic  19.9 us (2%)
  between operations  16.3 us (2%)
  matrix products  10.9 us (1%)
    all_to_all x1, waiting for transfers between devices, shards(): lax.all_to_all(pieces, 'dp', split_axis=0, concat_axis=0, tiled=True)  456 us
    reduce_scatter x1, waiting for transfers between devices, factor_sums(): lax.psum_scatter(output_part, 'dp', scatter_dimension=0, tiled=True)  199 us
    unnamed x4, waiting for transfers between devices  134 us
    all_gather x1, waiting for transfers between devices, shards(): lax.all_gather(inputs, 'tensor', axis=1, tiled=True)  48.5 us
    reshape x2, local copies, waits for them, and re-layouts, shards(): weight_grad.reshape(group_size, block_in, col_blocks, block_out)  28 us
  transfers between devices with their start and end apart: 7, of which 6 were waited for; matrix products, arithmetic and copies ran while one was open for 2% of the time, Pallas kernels for 0%

commit v1 on v0

v1 whole, which is shorter than its diff:
```python
import jax
import jax.numpy as jnp
import numpy as np
from jax import lax
from jax.experimental import pallas as pl
from jax.experimental.pallas import tpu as pltpu
from jax.sharding import PartitionSpec as P

MESH = pl.DeviceIdType.MESH
HIGHEST = lax.Precision.HIGHEST
F32 = jnp.float32
BF16 = jnp.bfloat16
Z = 16
HOPS = 8
NARROW = 4
TOTAL = 16384
STREAM_ROWS = (48, 80, 80)


def kernel(
    gate_ref, up_ref, cot_ref, xt_ref, sel_ref, left_ref, right_ref, pick_ref, owner_ref,
    input_ref, output_ref, pre_ref,
    xb, ib, gb, osum, isum, part, tile, fin, ret,
    rb0, rf0, sb0, sf0, rb1, rf1, sb1, sf1, rb2, rf2, sb2, sf2,
    y_s, y_r, x_s, x_r, cx_s, cx_r, gy_s, gy_r, gc_s, gc_r, rs_s, rs_r, d_s, d_r, dc_s, dc_r, t_s, t_r,
):
    dp = lax.axis_index("dp")
    tn = lax.axis_index("tensor")
    h, z, c = dp // 32, (dp // 2) % Z, dp % 2
    x, ylo = tn // 2, tn % 2
    y = h * 2 + ylo

    def dev(x_, y_, z_, c_):
        return ((y_ // 2) * 32 + z_ * 2 + c_, x_ * 2 + y_ % 2)

    xr, xl = (x + 1) % 4, (x + 3) % 4
    zr, zl = (z + 1) % Z, (z + Z - 1) % Z
    zx = z + 1 - 2 * (z % 2)
    sibling = dev(x, y, z, 1 - c)
    across = dev(x, (y + 2) % 4, z, c)
    right, left = dev(xr, y, z, c), dev(xl, y, z, c)
    up_z, down_z = dev(x, y, zr, c), dev(x, y, zl, c)
    diagonal = dev(x, (y + 2) % 4, zx, c)
    ring_y = [dev(x, (y + k) % 4, z, c) for k in (1, 2, 3)]

    barrier = pltpu.get_barrier_semaphore()
    peers = ring_y + [right, left, sibling, up_z, down_z, diagonal]
    for peer in peers:
        pl.semaphore_signal(barrier, inc=1, device_id=peer, device_id_type=MESH)
    pl.semaphore_wait(barrier, len(peers))

    sends = []

    def send(src, dst, s_sem, r_sem, to):
        copy = pltpu.make_async_remote_copy(
            src_ref=src, dst_ref=dst, send_sem=s_sem, recv_sem=r_sem, device_id=to, device_id_type=MESH
        )
        copy.start()
        sends.append(copy)

    def arrive(dst, s_sem, r_sem):
        pltpu.make_async_remote_copy(
            src_ref=dst, dst_ref=dst, send_sem=s_sem, recv_sem=r_sem, device_id=sibling, device_id_type=MESH
        ).wait_recv()

    for k in (1, 3):
        half = ((y + k) % 4) // 2
        send(xt_ref.at[half], xb.at[c, x, y], y_s.at[k], y_r.at[k], ring_y[k - 1])
    send(xt_ref, ib.at[c, h], y_s.at[2], y_r.at[2], across)
    xb[c, x, y] = xt_ref[h]
    ib[c, h] = xt_ref[...]

    for n in range(4):
        cols = slice(n * 256, n * 256 + 256)
        pre = gate_ref[:, cols].astype(F32)
        s = jax.nn.sigmoid(pre)
        slope = s * (1.0 + pre * (1.0 - s))
        gb[c, h, n] = (cot_ref[:, cols].astype(F32) * up_ref[:, cols].astype(F32) * slope).astype(BF16)
        mine = gb.at[c, h, n]
        send(mine, mine, gy_s.at[n], gy_r.at[n], across)
        send(mine, mine, gc_s.at[n], gc_r.at[n], sibling)

    for k in (1, 3):
        arrive(xb.at[c, x, (y + 4 - k) % 4], y_s.at[k], y_r.at[k])
    arrive(ib.at[c, 1 - h], y_s.at[2], y_r.at[2])
    xb[c, x, (y + 2) % 4] = ib[c, 1 - h, h]
    own = xb.at[c, x]
    send(own, own, x_s.at[0], x_r.at[0], right)
    send(own, own, x_s.at[1], x_r.at[1], left)
    send(own, own, cx_s.at[0], cx_r.at[0], sibling)
    send(ib.at[c], ib.at[c], cx_s.at[4], cx_r.at[4], sibling)

    from_l, from_r, far = xb.at[c, xl], xb.at[c, xr], (x + 2) % 4
    arrive(from_l, x_s.at[0], x_r.at[0])
    low = xb.at[c, xl, pl.ds(0, 2)]
    send(low, low, x_s.at[2], x_r.at[2], right)
    arrive(from_r, x_s.at[1], x_r.at[1])
    high = xb.at[c, xr, pl.ds(2, 2)]
    send(high, high, x_s.at[3], x_r.at[3], left)
    send(from_l, from_l, cx_s.at[1], cx_r.at[1], sibling)
    send(from_r, from_r, cx_s.at[2], cx_r.at[2], sibling)

    for n in range(4):
        other = gb.at[c, 1 - h, n]
        arrive(other, gy_s.at[n], gy_r.at[n])
        send(other, other, gc_s.at[4 + n], gc_r.at[4 + n], sibling)
    for n in range(4):
        arrive(gb.at[1 - c, h, n], gc_s.at[n], gc_r.at[n])
    for n in range(4):
        arrive(gb.at[1 - c, 1 - h, n], gc_s.at[4 + n], gc_r.at[4 + n])
    arrive(ib.at[1 - c], cx_s.at[4], cx_r.at[4])

    for i in range(2):
        for j in range(2):
            total = jnp.zeros((256, 256), F32)
            for k in range(2):
                for m in range(2):
                    total += lax.dot_general(
                        gb[k, m, 2 * h + i], gb[k, m, 2 * h + j],
                        (((0,), (0,)), ((), ())), preferred_element_type=F32,
                    )
            osum[pl.ds(i * 256, 256), pl.ds(j * 256, 256)] = total
    isum[...] = jnp.zeros_like(isum)
    for half in range(2):
        total = jnp.zeros((256, 160), F32)
        for k in range(2):
            for m in range(2):
                rows = jnp.dot(sel_ref[...], ib[k, m, h], preferred_element_type=F32).astype(BF16)
                total += lax.dot_general(
                    rows, ib[k, m, half], (((1,), (1,)), ((), ())), preferred_element_type=F32
                )
        isum[:, half * 160:half * 160 + 160] = total

    arrive(xb.at[c, far, pl.ds(0, 2)], x_s.at[2], x_r.at[2])
    arrive(xb.at[c, far, pl.ds(2, 2)], x_s.at[3], x_r.at[3])
    send(xb.at[c, far], xb.at[c, far], cx_s.at[3], cx_r.at[3], sibling)
    for k, p in enumerate((x, xl, xr, far)):
        arrive(xb.at[1 - c, p], cx_s.at[k], cx_r.at[k])

    def partial_tile(t, slot):
        px, py, pc = pick_ref[0, t], pick_ref[1, t], pick_ref[2, t]
        total = jnp.zeros((160, 256), F32)
        for k in range(2):
            for m in range(2):
                total += jnp.dot(xb[k, px, 2 * m + py], gb[k, m, 2 * pc + c], preferred_element_type=F32)
        part[slot] = total

    def factor_rows(t):
        o_rows = pl.ds(pl.multiple_of(t * 32 + c * 16, 16), 16)
        i_rows = pl.ds(pl.multiple_of(t * 16 + c * 8, 8), 8)
        return jnp.concatenate(
            [osum[o_rows, 0:256], osum[o_rows, 256:512], isum[i_rows, 0:256], isum[i_rows, 256:512]], axis=0
        )

    bufs = ((rb0, rf0, sb0, sf0), (rb1, rf1, sb1, sf1), (rb2, rf2, sb2, sf2))

    def own_part(stream, t, slot):
        if stream == 0:
            return factor_rows(t)
        return part[slot, (stream - 1) * 80:(stream - 1) * 80 + 80]

    def landing(stream, way, step):
        rb, rf = bufs[stream][:2]
        return rb.at[way, step] if step < NARROW else rf.at[way, step - NARROW]

    def hop(stream, way, step, t, slot):
        value = own_part(stream, t, slot)
        if step > 0:
            came = landing(stream, way, step - 1)
            arrive(came, rs_s.at[stream, way, step - 1], rs_r.at[stream, way, step - 1])
            value = value + came[...].astype(F32)
        sb, sf = bufs[stream][2:]
        out = sb.at[way, step] if step < NARROW else sf.at[way, step - NARROW]
        out[...] = value.astype(out.dtype)
        send(out, landing(stream, way, step), rs_s.at[stream, way, step], rs_r.at[stream, way, step],
             up_z if way == 0 else down_z)

    def target(way, step):
        return (z + 7 - step) % Z if way == 0 else (z + 8 + step) % Z

    lengths = (7, 8)
    for step in range(HOPS):
        for way in range(2):
            if step < lengths[way]:
                partial_tile(target(way, step), (step % 2) * 2 + way)
        for stream in range(3):
            for way in range(2):
                if step < lengths[way]:
                    hop(stream, way, step, target(way, step), (step % 2) * 2 + way)
    partial_tile(z, 0)

    def finish(stream):
        value = own_part(stream, z, 0)
        for way in range(2):
            last = lengths[way] - 1
            came = landing(stream, way, last)
            arrive(came, rs_s.at[stream, way, last], rs_r.at[stream, way, last])
            value = value + came[...].astype(F32)
        return value * (1.0 / TOTAL)

    factors = finish(0)
    output_ref[:, 0:256] = factors[0:16]
    output_ref[:, 256:512] = factors[16:32]
    input_ref[:, 0:256] = factors[32:37]
    input_ref[:, 256:320] = factors[40:45, 0:64]

    goes = z % 2
    stays = h == goes
    done = sb_tile = tile.at[2]
    done[c, 0:80] = finish(1).astype(BF16)
    done[c, 80:160] = finish(2).astype(BF16)
    mine = tile.at[2, c]
    send(mine, tile.at[h, c], d_s.at[0], d_r.at[h], dev(x, goes * 2 + ylo, zx, c))

    @pl.when(stays)
    def _():
        tile[h, c] = tile[2, c]

    @pl.when(jnp.logical_not(stays))
    def _():
        pltpu.make_async_remote_copy(
            src_ref=mine, dst_ref=tile.at[h, c], send_sem=d_s.at[1], recv_sem=d_r.at[h],
            device_id=across, device_id_type=MESH,
        ).start()
        arrive(tile.at[h, c], d_s.at[0], d_r.at[h])

    arrive(tile.at[1 - h, c], d_s.at[0], d_r.at[1 - h])
    for k in range(2):
        send(tile.at[k, c], tile.at[k, c], dc_s.at[k], dc_r.at[k], sibling)
    for k in range(2):
        arrive(tile.at[k, 1 - c], dc_s.at[k], dc_r.at[k])

    right_all = right_ref[...]
    right_hi = right_all.astype(BF16)
    right_lo = (right_all - right_hi.astype(F32)).astype(BF16)
    for k in range(2):
        total = jnp.zeros((160, 128), F32)
        for m in range(2):
            piece = tile[k, m]
            rows = slice(m * 256, m * 256 + 256)
            total += jnp.dot(piece, right_hi[rows], preferred_element_type=F32)
            total += jnp.dot(piece, right_lo[rows], preferred_element_type=F32)
        part[0, k * 80:k * 80 + 80, 0:128] = total[0:80]
        part[0, k * 80:k * 80 + 80, 128:256] = total[80:160]
    right_part = jnp.concatenate(
        [part[0, 0:80, 0:128], part[0, 0:80, 128:256], part[0, 80:160, 0:128], part[0, 80:160, 128:256]], axis=0
    )
    finished = jnp.dot(left_ref[...], right_part, precision=HIGHEST, preferred_element_type=F32)
    fin[...] = finished.reshape(320, 1, 128)

    def back(i, _):
        to = lax.rem(dp + i, 64)
        pltpu.make_async_remote_copy(
            src_ref=fin.at[pl.ds(to * 5, 5)], dst_ref=ret.at[pl.ds(dp * 5, 5)],
            send_sem=t_s.at[to], recv_sem=t_r.at[dp], device_id=(to, tn), device_id_type=MESH,
        ).start()
        return 0

    lax.fori_loop(1, 64, back, 0)
    ret[pl.ds(dp * 5, 5)] = fin[pl.ds(dp * 5, 5)]

    def back_wait(i, _):
        to = lax.rem(dp + i, 64)
        copy = pltpu.make_async_remote_copy(
            src_ref=fin.at[pl.ds(to * 5, 5)], dst_ref=ret.at[pl.ds(to * 5, 5)],
            send_sem=t_s.at[to], recv_sem=t_r.at[to], device_id=(to, tn), device_id_type=MESH,
        )
        copy.wait_recv()
        copy.wait_send()
        return 0

    lax.fori_loop(1, 64, back_wait, 0)
    for a in range(8):
        for b in range(2):
            first = owner_ref[0, a * 2 + b] * 20
            for w in range(4):
                col = b * 512 + w * 128
                pre_ref[a, :, col:col + 128] = ret[pl.ds(first + w * 5, 5)].reshape(5, 128)

    for copy in sends:
        copy.wait_send()

    @pl.when(jnp.logical_not(stays))
    def _():
        pltpu.make_async_remote_copy(
            src_ref=mine, dst_ref=tile.at[h, c], send_sem=d_s.at[1], recv_sem=d_r.at[h],
            device_id=across, device_id_type=MESH,
        ).wait_send()


def selection():
    sel = np.zeros((256, 160), np.float32)
    for g in range(32):
        for i in range(5):
            sel[8 * g + i, 5 * g + i] = 1.0
    return sel


def shards(inputs, gate_values, up_values, hidden_cotangent, owners, left_inverse, right_inverse):
    xt = inputs.T.reshape(2, 160, 256)
    owner_row = owners[0]
    tiles = jnp.arange(16, dtype=jnp.int32)
    slots = (tiles % 2) * 8 + tiles // 2
    held = jnp.sum(jnp.where(owner_row[None, :] == slots[:, None], tiles[None, :], 0), axis=1)
    pick = jnp.stack([held // 4, (held // 2) % 2, held % 2])
    vmem = pl.BlockSpec(memory_space=pltpu.VMEM)
    smem = pl.BlockSpec(memory_space=pltpu.SMEM)
    scratch = [
        pltpu.VMEM((2, 4, 4, 160, 256), BF16),
        pltpu.VMEM((2, 2, 2, 160, 256), BF16),
        pltpu.VMEM((2, 2, 4, 256, 256), BF16),
        pltpu.VMEM((512, 512), F32),
        pltpu.VMEM((256, 512), F32),
        pltpu.VMEM((4, 160, 256), F32),
        pltpu.VMEM((3, 2, 160, 256), BF16),
        pltpu.VMEM((320, 1, 128), F32),
        pltpu.VMEM((320, 1, 128), F32),
    ]
    for rows in STREAM_ROWS:
        for _ in range(2):
            scratch.append(pltpu.VMEM((2, NARROW, rows, 256), BF16))
            scratch.append(pltpu.VMEM((2, HOPS - NARROW, rows, 256), F32))
    dma = pltpu.SemaphoreType.DMA
    for shape in ((4,), (4,), (4,), (4,), (5,), (5,), (4,), (4,), (8,), (8,), (3, 2, HOPS), (3, 2, HOPS),
                  (2,), (2,), (2,), (2,), (64,), (64,)):
        scratch.append(dma(shape))
    input_rows, output_rows, pre = pl.pallas_call(
        kernel,
        out_shape=(
            jax.ShapeDtypeStruct((5, 320), F32),
            jax.ShapeDtypeStruct((16, 512), F32),
            jax.ShapeDtypeStruct((8, 5, 1024), F32),
        ),
        in_specs=[vmem] * 7 + [smem] * 2,
        out_specs=(vmem, vmem, vmem),
        scratch_shapes=scratch,
        compiler_params=pltpu.CompilerParams(
            collective_id=0, has_side_effects=True, vmem_limit_bytes=48 * 2**20
        ),
        name="kfac",
    )(
        gate_values, up_values, hidden_cotangent, xt, jnp.asarray(selection(), BF16),
        left_inverse[0, 0], right_inverse[0, 0], pick, owners,
    )
    return input_rows[None], output_rows[None], pre


def solution(mesh):
    in_specs = (
        P("dp", "tensor"), P("dp", "tensor"), P("dp", "tensor"), P("dp", "tensor"), P("tensor", None),
        P("dp", "tensor", None, None), P("dp", "tensor", None, None),
    )
    out_specs = (P("tensor", "dp", None), P("tensor", "dp", None), P(None, "dp", "tensor"))
    return jax.shard_map(shards, mesh=mesh, in_specs=in_specs, out_specs=out_specs, check_vma=False)
```

time: 992 us -> 110 us (0.11); the launches traced: 980 us -> 110 us
  waiting for transfers between devices: 843 us -> 0 us
  Pallas kernels: 0 us -> 99.5 us
  local copies, waits for them, and re-layouts: 52.5 us -> 9.54 us
  starting transfers between devices: 37.3 us -> 0 us
  other arithmetic: 19.9 us -> 0.22 us
  between operations: 16.3 us -> 0.68 us
  matrix products: 10.9 us -> 0 us
    all_to_all x2 -> x0, waiting for transfers between devices: 456 us -> none  [the longest x1 456 us: shards(): lax.all_to_all(pieces, 'dp', split_axis=0, concat_axis=0, tiled=True)]
    reduce_scatter x1 -> x0, waiting for transfers between devices: 199 us -> none  [factor_sums(): lax.psum_scatter(output_part, 'dp', scatter_dimension=0, tiled=True)]
    unnamed x4 -> x0, waiting for transfers between devices: 134 us -> none
    pallas_call x0 -> x1, Pallas kernels: none -> 99.5 us  [shards(): pl.pallas_call(kernel, out_shape=(jax.ShapeDtypeStruct((5, 320), F32), ja...]
    all_gather x1 -> x0, waiting for transfers between devices: 48.5 us -> none  [shards(): lax.all_gather(inputs, 'tensor', axis=1, tiled=True)]
    all_to_all x2 -> x0, starting transfers between devices: 28.9 us -> none  [the longest x1 19.8 us: shards(): lax.all_to_all(pieces, 'dp', split_axis=0, concat_axis=0, tiled=True)]
    reshape x4 -> x0, local copies, waits for them, and re-layouts: 28.8 us -> none  [the longest x2 28 us: shards(): weight_grad.reshape(group_size, block_in, col_blocks, block_out)]
    dot_general x5 -> x0, matrix products: 10.9 us -> none  [the longest x1 6.81 us: shards(): lax.dot_general(lax.all_gather(inputs, 'tensor', axis=1, tiled=True), gat...]
  transfers between devices with their start and end apart: 7 -> 0, of which waited for: 6 -> 0; matrix products, arithmetic and copies ran while one was open for 2% -> 0% of each run, Pallas kernels for 0% -> 0%
where the time goes in v1:
time: 110 us
  Pallas kernels  99.5 us (90%)
  local copies, waits for them, and re-layouts  9.54 us (9%)
    pallas_call x1, Pallas kernels, shards(): pl.pallas_call(kernel, out_shape=(jax.ShapeDtypeStruct((5, 320), F32), ja...  99.5 us
    unnamed x19, local copies, waits for them, and re-layouts  9.54 us

profile of v1, /device:TPU:1, one launch (start us, length us, event | category | flops | bytes accessed | tf_op | source)
XLA Modules:
  0.0 109.9 jit_solution(17463491647579415541)
XLA Ops:
  0.6 0.0 copy-start.7
  0.7 0.6 copy-done.7
  1.3 0.2 select_reduce_fusion
  1.5 0.0 copy-start
  1.5 1.0 copy-done
  2.6 0.0 copy-start.1
  2.6 1.0 copy-done.1
  3.6 0.0 copy-start.2
  3.6 1.0 copy-done.2
  4.6 0.0 copy-start.3
  4.6 1.0 copy-done.3
  5.7 0.0 copy-start.4
  5.7 0.9 copy-done.4
  6.6 0.0 copy-start.5
  6.6 0.9 copy-done.5
  7.5 0.0 copy-start.6
  7.5 0.9 copy-done.6
  8.4 99.5 %kfac.1 = (f32[5,320]{1,0:T(8,128)S(1)}, f32[16,512]{1,0:T(8,128)S(1)}, f32[8,5,1024]{2,1,0:T(8,128)S(1)}) custom-call(bf16[256,1024]{1,0:T(8,128)(2,1)S(1)} %copy-done, bf16[256,1024]{1,0:T(8,128)(2,1)S(1)} %copy-done.1, bf16[256,1024]{1,0:T(8,128)(2,1)S(1)} %copy-done.2, bf16[2,160,256]{2,1,0:T(8,128)(2,1)S(1)} %bitcast.30, ...), custom_call_target="tpu_custom_call" | custom-call | tf_op jit(solution)/shard_map/kfac/pallas_call | solution.py:327
  108.0 0.6 copy.13
  108.6 0.8 copy.14
  109.3 0.6 copy.16
  (3 shorter events, 0.0 us)
Async XLA Ops:
  0.6 0.7 copy-start.7
  1.5 1.0 copy-start
  2.6 1.0 copy-start.1
  3.6 1.0 copy-start.2
  4.6 1.0 copy-start.3
  5.7 0.9 copy-start.4
  6.6 0.9 copy-start.5
  7.5 0.9 copy-start.6

commit v2 on v1

v2 whole, which is shorter than its diff:
```python
import jax
import jax.numpy as jnp
from jax import lax
from jax.experimental import pallas as pl
from jax.experimental.pallas import tpu as pltpu
from jax.sharding import PartitionSpec as P

MESH = pl.DeviceIdType.MESH
F32 = jnp.float32
BF16 = jnp.bfloat16
Z = 16
REACH = 4
ORDER = (8, 7, 3, 6, 2, 5, 1, 4)
TOTAL = 16384
LEAD = 3
STREAM_ROWS = (80, 80, 80)
STREAM_FIRST = (0, 0, 80)
STREAM_LANES = (128, 256, 256)
LONG_WAY = (0, 0, 1)
TILE_STREAMS = tuple(range(1, len(STREAM_ROWS)))


def split(value):
    high = value.astype(BF16)
    return high, (value - high.astype(F32)).astype(BF16)


def dot3(a, b):
    (a_hi, a_lo), (b_hi, b_lo) = a, b
    total = jnp.dot(a_hi, b_hi, preferred_element_type=F32)
    total += jnp.dot(a_hi, b_lo, preferred_element_type=F32)
    return total + jnp.dot(a_lo, b_hi, preferred_element_type=F32)


def kernel(
    gate_in, up_in, cot_in, xt_in, left_in, right_in, owner_in,
    input_ref, output_ref, pre_ref,
    gates, owner_ref, left_ref, rb, rsplit, lsplit,
    xb, ib, gb, osum, isum, part, piece, rpart, worker_part, fin, ret,
    ring,
    l_s, y_s, y_r, x_s, x_r, cx_s, cx_r, gy_s, gy_r, gc_s, gc_r, r_s, r_r,
    rs_s, rs_r, p_s, p_r, d_s, d_r, t_s, t_r,
):
    dp = lax.axis_index("dp")
    tn = lax.axis_index("tensor")
    h, z, c = dp // 32, (dp // 2) % Z, dp % 2
    x, ylo = tn // 2, tn % 2
    y = h * 2 + ylo
    zbit = z % 2
    home = h == zbit
    away = jnp.logical_not(home)

    def dev(x_, y_, z_, c_):
        return ((y_ // 2) * 32 + z_ * 2 + c_, x_ * 2 + y_ % 2)

    xr, xl, far = (x + 1) % 4, (x + 3) % 4, (x + 2) % 4
    zx = z + 1 - 2 * zbit
    sibling = dev(x, y, z, 1 - c)
    across = dev(x, (y + 2) % 4, z, c)
    right, left = dev(xr, y, z, c), dev(xl, y, z, c)
    step_z = (dev(x, y, (z + 1) % Z, c), dev(x, y, (z + Z - 1) % Z, c))
    leap_z = (dev(x, y, (z + REACH) % Z, c), dev(x, y, (z + Z - REACH) % Z, c))
    pair_z = dev(x, y, zx, c)
    diagonal = dev(x, (y + 2) % 4, zx, c)
    ring_y = [dev(x, (y + k) % 4, z, c) for k in (1, 2, 3)]

    barrier = pltpu.get_barrier_semaphore()
    peers = ring_y + [right, left, sibling, diagonal, *step_z, *leap_z]
    for peer in peers:
        pl.semaphore_signal(barrier, inc=1, device_id=peer, device_id_type=MESH)

    loads = [
        pltpu.make_async_copy(src, dst, l_s.at[k])
        for k, (src, dst) in enumerate((
            (xt_in.at[h], xb.at[c, x, y]), (xt_in, ib.at[c, h]),
            (gate_in, gates.at[0]), (up_in, gates.at[1]), (cot_in, gates.at[2]),
            (owner_in, owner_ref), (left_in, left_ref),
        ))
    ]
    for load in loads:
        load.start()

    def right_slot(which):
        return rb.at[:, pl.ds(pl.multiple_of(which * 128, 128), 128)]

    right_load = pltpu.make_async_copy(right_in, right_slot(zbit), l_s.at[7])
    pl.when(home)(right_load.start)
    pl.semaphore_wait(barrier, len(peers))

    sends = []

    def remote(src, dst, s_sem, r_sem, to):
        return pltpu.make_async_remote_copy(
            src_ref=src, dst_ref=dst, send_sem=s_sem, recv_sem=r_sem, device_id=to, device_id_type=MESH
        )

    def send(src, dst, s_sem, r_sem, to):
        copy = remote(src, dst, s_sem, r_sem, to)
        copy.start()
        sends.append(copy)

    def arrive(dst, s_sem, r_sem):
        remote(dst, dst, s_sem, r_sem, sibling).wait_recv()

    for k in (1, 3):
        half = ((y + k) % 4) // 2
        send(xt_in.at[half], xb.at[c, x, y], y_s.at[k], y_r.at[k], ring_y[k - 1])
    send(xt_in, ib.at[c, h], y_s.at[2], y_r.at[2], across)
    right_away = remote(right_in, right_slot(zbit), r_s.at[0], r_r.at[0], pair_z)
    pl.when(away)(right_away.start)

    def quarter(p, block):
        return 2 * block + p % 2

    for load in loads[2:5]:
        load.wait()
    for p in range(4):
        n = quarter(p, 1 - h if p < 2 else h)
        cols = pl.ds(pl.multiple_of(n * 256, 256), 256)
        pre = gates[0, :, cols].astype(F32)
        s = jax.nn.sigmoid(pre)
        slope = s * (1.0 + pre * (1.0 - s))
        gb[c, h, n] = (gates[2, :, cols].astype(F32) * gates[1, :, cols].astype(F32) * slope).astype(BF16)
        mine = gb.at[c, h, n]
        send(mine, mine, gy_s.at[p], gy_r.at[p], across)
        send(mine, mine, gc_s.at[p], gc_r.at[p], sibling)
    loads[0].wait()
    loads[1].wait()

    for k in (1, 3):
        arrive(xb.at[c, x, (y + 4 - k) % 4], y_s.at[k], y_r.at[k])
    arrive(ib.at[c, 1 - h], y_s.at[2], y_r.at[2])
    xb[c, x, (y + 2) % 4] = ib[c, 1 - h, h]

    def pieces(core, place, k):
        return xb.at[core, place, pl.ds(2 * k, 2)]

    own = (pieces(c, x, 0), pieces(c, x, 1))
    send(own[0], own[0], x_s.at[0], x_r.at[0], right)
    send(own[1], own[1], x_s.at[1], x_r.at[1], left)
    send(own[1], own[1], x_s.at[2], x_r.at[2], right)
    send(own[0], own[0], x_s.at[3], x_r.at[3], left)
    send(xb.at[c, x], xb.at[c, x], cx_s.at[0], cx_r.at[0], sibling)
    send(ib.at[c], ib.at[c], cx_s.at[4], cx_r.at[4], sibling)

    low, high = pieces(c, xl, 0), pieces(c, xr, 1)
    arrive(low, x_s.at[0], x_r.at[0])
    send(low, low, x_s.at[4], x_r.at[4], right)
    arrive(high, x_s.at[1], x_r.at[1])
    send(high, high, x_s.at[5], x_r.at[5], left)

    def pass_gate(p):
        n = quarter(p, h if p < 2 else 1 - h)
        other = gb.at[c, 1 - h, n]
        arrive(other, gy_s.at[p], gy_r.at[p])
        send(other, other, gc_s.at[4 + p], gc_r.at[4 + p], sibling)

    def gate_passed(p):
        arrive(gb.at[1 - c, h, quarter(p, 1 - h if p < 2 else h)], gc_s.at[p], gc_r.at[p])
        arrive(gb.at[1 - c, 1 - h, quarter(p, h if p < 2 else 1 - h)], gc_s.at[4 + p], gc_r.at[4 + p])

    pass_gate(0)
    pass_gate(1)
    arrive(ib.at[1 - c], cx_s.at[4], cx_r.at[4])

    row = lax.broadcasted_iota(jnp.int32, (256, 160), 0)
    col = lax.broadcasted_iota(jnp.int32, (256, 160), 1)
    start = (row >> 4) * 10 + c * 5
    parts = []
    for b in range(3):
        at = (row & 15) - 5 * b
        parts.append(((col == start + at) & (at >= 0) & (at < 5)).astype(F32).astype(BF16))
    total = jnp.zeros((256, 128), F32)
    for k in range(2):
        for m in range(2):
            features = ib[k, m].reshape(320, 256)
            for b in range(3):
                rows = jnp.dot(parts[b], ib[k, m, h], preferred_element_type=F32).astype(BF16)
                columns = features[b * 128:min(b * 128 + 128, 320)]
                term = lax.dot_general(rows, columns, (((1,), (1,)), ((), ())), preferred_element_type=F32)
                if b == 2:
                    term = jnp.concatenate([term, jnp.zeros((256, 64), F32)], axis=1)
                total += term
    isum[...] = total

    for k in range(2):
        arrive(gb.at[1 - c, h, quarter(k, h)], gc_s.at[2 + k], gc_r.at[2 + k])
        arrive(gb.at[1 - c, 1 - h, quarter(k, h)], gc_s.at[4 + k], gc_r.at[4 + k])
    for i in range(2):
        for j in range(2):
            total = jnp.zeros((256, 256), F32)
            for k in range(2):
                for m in range(2):
                    total += lax.dot_general(
                        gb[k, m, 2 * h + i], gb[k, m, 2 * h + j],
                        (((0,), (0,)), ((), ())), preferred_element_type=F32,
                    )
            osum[pl.ds(i * 256, 256), pl.ds(j * 256, 256)] = total

    def held_tile(t):
        slot = (t % 2) * 8 + t // 2
        held = jnp.int32(0)
        for k in range(16):
            held = jnp.maximum(held, jnp.where(owner_ref[0, k] == slot, k, 0))
        return held

    def partial_tile(t, slot):
        held = held_tile(t)
        px, py, pc = held >> 2, (held >> 1) & 1, held & 1
        total = jnp.zeros((160, 256), F32)
        for k in range(2):
            for m in range(2):
                total += jnp.dot(xb[k, px, 2 * m + py], gb[k, m, 2 * pc + c], preferred_element_type=F32)
        part[slot] = total

    def factor_rows(t):
        o_rows = pl.ds(pl.multiple_of(t * 32 + c * 16, 16), 16)
        i_rows = pl.ds(pl.multiple_of(t * 16, 16), 16)
        return jnp.concatenate(
            [osum[o_rows, k * 128:k * 128 + 128] for k in range(4)] + [isum[i_rows, :]], axis=0
        )


    def target(way, distance):
        return (z + distance) % Z if way == 0 else (z + Z - distance) % Z

    def place(index, way):
        return 0 if index == 0 else (index % 2) * 2 + way

    def own_part(stream, index, way):
        if stream == 0:
            return factor_rows(target(way, ORDER[index] if index < 8 else 0))
        return part[place(index, way), pl.ds(STREAM_FIRST[stream], STREAM_ROWS[stream])]

    def landed(stream, way, distance):
        came = ring[stream][0].at[way, distance - 1]
        arrive(came, rs_s.at[stream, way, distance - 1], rs_r.at[stream, way, distance - 1])
        return came[...].astype(F32)

    def hop(stream, index):
        distance = ORDER[index]
        for way in range(2):
            farthest = 8 if way == LONG_WAY[stream] else 7
            if distance > farthest:
                continue
            value = own_part(stream, index, way)
            if distance not in (farthest, REACH - 1):
                value = value + landed(stream, way, distance + 1)
            out = ring[stream][1].at[way, distance - 1]
            out[...] = value.astype(BF16)
            to = leap_z if distance == REACH else step_z
            send(out, ring[stream][0].at[way, distance - 1], rs_s.at[stream, way, distance - 1],
                 rs_r.at[stream, way, distance - 1], to[way])

    def finish(stream):
        value = own_part(stream, 8, 0)
        for distance in (1, REACH):
            for way in range(2):
                value = value + landed(stream, way, distance)
        return value * (1.0 / TOTAL)

    hop(0, 0)
    arrive(pieces(c, xl, 1), x_s.at[2], x_r.at[2])
    send(xb.at[c, xl], xb.at[c, xl], cx_s.at[1], cx_r.at[1], sibling)
    arrive(pieces(c, xr, 0), x_s.at[3], x_r.at[3])
    send(xb.at[c, xr], xb.at[c, xr], cx_s.at[2], cx_r.at[2], sibling)
    hop(0, 1)
    pass_gate(2)
    pass_gate(3)
    hop(0, 2)
    arrive(pieces(c, far, 0), x_s.at[4], x_r.at[4])
    arrive(pieces(c, far, 1), x_s.at[5], x_r.at[5])
    send(xb.at[c, far], xb.at[c, far], cx_s.at[3], cx_r.at[3], sibling)
    loads[5].wait()
    for k in range(2):
        arrive(gb.at[1 - c, h, quarter(k, 1 - h)], gc_s.at[k], gc_r.at[k])
        arrive(gb.at[1 - c, 1 - h, quarter(k, 1 - h)], gc_s.at[6 + k], gc_r.at[6 + k])
    for k, at in enumerate((x, xl, xr, far)):
        arrive(xb.at[1 - c, at], cx_s.at[k], cx_r.at[k])

    right_on = remote(rb, rb, r_s.at[1], r_r.at[1], across)

    for step in range(8):
        if step == 0:
            partial_tile(target(0, ORDER[0]), 0)
        ahead = [(step + 1, way) for way in range(2 if step < 7 else 1)]
        for k, stream in enumerate(TILE_STREAMS):
            hop(stream, step)
            if k % (len(TILE_STREAMS) // 2) == 0 and ahead:
                to, way = ahead.pop(0)
                partial_tile(target(way, ORDER[to] if to < 8 else 0), place(to, way))
        if step + LEAD < 8:
            hop(0, step + LEAD)
        if step == 0:
            @pl.when(home)
            def _():
                right_load.wait()
                arrive(right_slot(1 - zbit), r_s.at[0], r_r.at[0])
                right_on.start()
            loads[6].wait()
            lsplit[0], lsplit[1] = split(left_ref[...])
        if step == 5:
            pl.when(away)(right_on.wait_recv)
            rsplit[0], rsplit[1] = split(rb[...])
            factors = finish(0)
            for k in range(4):
                output_ref[:, k * 128:k * 128 + 128] = factors[k * 16:k * 16 + 16]
            input_ref[:, 0:128] = factors[64:69]
            input_ref[:, 128:256] = factors[69:74]
            input_ref[:, 256:320] = factors[74:79, 0:64]

    for i in range(2):
        for stream in TILE_STREAMS:
            first = STREAM_FIRST[stream] - i * 80
            if 0 <= first < 80:
                piece[c, i, pl.ds(first, STREAM_ROWS[stream])] = finish(stream)
        mine = piece.at[c, i]
        send(mine, mine, p_s.at[i], p_r.at[i], sibling)
    goes = dev(x, zbit * 2 + ylo, zx, c)
    stay_copies = []
    for i in range(2):
        arrive(piece.at[1 - c, i], p_s.at[i], p_r.at[i])
        total = jnp.zeros((80, 256), F32)
        for k in range(2):
            rows = slice(k * 256, k * 256 + 256)
            total += dot3(split(piece[k, i]), (rsplit[0, rows], rsplit[1, rows]))
        rpart[0, i] = total[:, 0:128]
        rpart[1, i] = total[:, 128:256]
        send(rpart.at[1 - zbit, i], worker_part.at[h, i], d_s.at[i], d_r.at[h, i], goes)
        stay_copies.append(remote(rpart.at[zbit, i], worker_part.at[h, i], d_s.at[2 + i], d_r.at[h, i], across))
        pl.when(away)(stay_copies[i].start)

    @pl.when(home)
    def _():
        worker_part[h] = rpart[zbit]

    for i in range(2):
        @pl.when(away)
        def _():
            arrive(worker_part.at[h, i], d_s.at[i], d_r.at[h, i])
        arrive(worker_part.at[1 - h, i], d_s.at[i], d_r.at[1 - h, i])
    right_part = worker_part[...].reshape(320, 128)
    finished = dot3((lsplit[0], lsplit[1]), split(right_part))
    fin[...] = finished.reshape(320, 1, 128)

    def back_copy(to, at):
        return remote(fin.at[pl.ds(to * 5, 5)], ret.at[pl.ds(at * 5, 5)], t_s.at[to], t_r.at[at], (to, tn))

    def back(i, _):
        back_copy(lax.rem(dp + i, 64), dp).start()
        return 0

    lax.fori_loop(1, 64, back, 0)
    ret[pl.ds(dp * 5, 5)] = fin[pl.ds(dp * 5, 5)]

    def back_wait(i, _):
        to = lax.rem(dp + i, 64)
        copy = back_copy(to, to)
        copy.wait_recv()
        copy.wait_send()
        return 0

    lax.fori_loop(1, 64, back_wait, 0)
    for a in range(8):
        for b in range(2):
            first = jnp.clip(owner_ref[0, a * 2 + b], 0, 15) * 20
            for w in range(4):
                at = b * 512 + w * 128
                pre_ref[:, a:a + 1, at:at + 128] = ret[pl.ds(first + w * 5, 5)]

    for copy in sends:
        copy.wait_send()

    @pl.when(home)
    def _():
        right_on.wait_send()

    @pl.when(away)
    def _():
        right_away.wait_send()
        for copy in stay_copies:
            copy.wait_send()


def shards(inputs, gate_values, up_values, hidden_cotangent, owners, left_inverse, right_inverse):
    xt = inputs.T.reshape(2, 160, 256)
    vmem = pl.BlockSpec(memory_space=pltpu.VMEM)
    hbm = pl.BlockSpec(memory_space=pltpu.HBM)
    scratch = [
        pltpu.VMEM((3, 256, 1024), BF16),
        pltpu.SMEM((1, 16), jnp.int32),
        pltpu.VMEM((320, 320), F32),
        pltpu.VMEM((512, 256), F32),
        pltpu.VMEM((2, 512, 256), BF16),
        pltpu.VMEM((2, 320, 320), BF16),
        pltpu.VMEM((2, 4, 4, 160, 256), BF16),
        pltpu.VMEM((2, 2, 2, 160, 256), BF16),
        pltpu.VMEM((2, 2, 4, 256, 256), BF16),
        pltpu.VMEM((512, 512), F32),
        pltpu.VMEM((256, 128), F32),
        pltpu.VMEM((4, 160, 256), F32),
        pltpu.VMEM((2, 2, 80, 256), F32),
        pltpu.VMEM((2, 2, 80, 128), F32),
        pltpu.VMEM((2, 2, 80, 128), F32),
        pltpu.VMEM((320, 1, 128), F32),
        pltpu.VMEM((320, 1, 128), F32),
    ]
    scratch.append([
        [pltpu.VMEM((2, 8, rows, lanes), BF16)] * 2
        for rows, lanes in zip(STREAM_ROWS, STREAM_LANES)
    ])
    dma = pltpu.SemaphoreType.DMA
    for shape in ((8,), (4,), (4,), (6,), (6,), (5,), (5,), (4,), (4,), (8,), (8,), (2,), (2,),
                  (len(STREAM_ROWS), 2, 8), (len(STREAM_ROWS), 2, 8), (2,), (2,), (4,), (2, 2), (64,), (64,)):
        scratch.append(dma(shape))
    input_rows, output_rows, pre = pl.pallas_call(
        kernel,
        out_shape=(
            jax.ShapeDtypeStruct((5, 320), F32),
            jax.ShapeDtypeStruct((16, 512), F32),
            jax.ShapeDtypeStruct((5, 8, 1024), F32),
        ),
        in_specs=[hbm] * 7,
        out_specs=(vmem, vmem, vmem),
        scratch_shapes=scratch,
        compiler_params=pltpu.CompilerParams(
            collective_id=0, has_side_effects=True, vmem_limit_bytes=62 * 2**20
        ),
        name="kfac",
    )(
        gate_values, up_values, hidden_cotangent, xt, left_inverse[0, 0], right_inverse[0, 0], owners,
    )
    return input_rows[None], output_rows[None], pre.transpose(1, 0, 2)


def solution(mesh):
    in_specs = (
        P("dp", "tensor"), P("dp", "tensor"), P("dp", "tensor"), P("dp", "tensor"), P("tensor", None),
        P("dp", "tensor", None, None), P("dp", "tensor", None, None),
    )
    out_specs = (P("tensor", "dp", None), P("tensor", "dp", None), P(None, "dp", "tensor"))
    return jax.shard_map(shards, mesh=mesh, in_specs=in_specs, out_specs=out_specs, check_vma=False)
```

time: 110 us -> 102 us (0.927)
  local copies, waits for them, and re-layouts: 9.54 us -> 4.27 us
  Pallas kernels: 99.5 us -> 96.6 us
    unnamed x19 -> x3, local copies, waits for them, and re-layouts: 9.54 us -> 4.27 us
    pallas_call x1, Pallas kernels: 99.5 us -> 96.6 us  [shards(): pl.pallas_call(kernel, out_shape=(jax.ShapeDtypeStruct((5, 320), F32), ja...]
where the time goes in v2:
time: 102 us
  Pallas kernels  96.6 us (95%)
  local copies, waits for them, and re-layouts  4.27 us (4%)
    pallas_call x1, Pallas kernels, shards(): pl.pallas_call(kernel, out_shape=(jax.ShapeDtypeStruct((5, 320), F32), ja...  96.6 us
    unnamed x3, local copies, waits for them, and re-layouts  4.27 us

profile of v2, /device:TPU:1, one launch (start us, length us, event | category | flops | bytes accessed | tf_op | source)
XLA Modules:
  0.0 101.5 jit_solution(404662188019241083)
XLA Ops:
  0.6 96.6 %kfac.1 = (f32[5,320]{1,0:T(8,128)}, f32[16,512]{1,0:T(8,128)}, f32[5,8,1024]{2,1,0:T(8,128)}) custom-call(bf16[256,1024]{1,0:T(8,128)(2,1)} %gate_in.1, bf16[256,1024]{1,0:T(8,128)(2,1)} %up_in.1, bf16[256,1024]{1,0:T(8,128)(2,1)} %cot_in.1, bf16[2,160,256]{2,1,0:T(8,128)(2,1)} %bitcast.11, f32[320,320]{1,0:T(8,128)} %bitcast.8, f32[512,128]{1,0:T(8,128)} %bitcast.9, ...), custom_call_target="tpu_custom_call" | custom-call | tf_op jit(solution)/shard_map/kfac/pallas_call | solution.py:416
  97.2 1.3 %copy.10 = f32[1,5,320]{2,0,1:T(1,128)} copy(f32[1,5,320]{2,1,0:T(8,128)} %bitcast.13) | data formatting | bytes 12800
  98.5 1.4 %copy.13 = f32[1,16,512]{2,1,0:T(8,128)} copy(f32[1,16,512]{2,1,0:T(8,128)} %bitcast.12) | data formatting | bytes 65536
  99.9 1.6 %copy.14 = f32[8,5,1024]{2,0,1:T(8,128)} copy(f32[8,5,1024]{2,0,1:T(8,128)} %bitcast.10) | data formatting | bytes 327680

commit v3 on v2

--- a/solution.py
+++ b/solution.py
@@ -36,9 +36,9 @@
     gate_in, up_in, cot_in, xt_in, left_in, right_in, owner_in,
     input_ref, output_ref, pre_ref,
     gates, owner_ref, left_ref, rb, rsplit, lsplit,
-    xb, ib, gb, osum, isum, part, piece, rpart, worker_part, fin, ret,
+    xb, ib, gb, relay, osum, isum, part, piece, rpart, worker_part, fin, ret,
     ring,
-    l_s, y_s, y_r, x_s, x_r, cx_s, cx_r, gy_s, gy_r, gc_s, gc_r, r_s, r_r,
+    l_s, y_s, y_r, x_s, x_r, cx_s, cx_r, gr_s, gr_r, gy_s, gy_r, gc_s, gc_r, r_s, r_r,
     rs_s, rs_r, p_s, p_r, d_s, d_r, t_s, t_r,
 ):
     dp = lax.axis_index("dp")
@@ -102,10 +102,9 @@
     def arrive(dst, s_sem, r_sem):
         remote(dst, dst, s_sem, r_sem, sibling).wait_recv()
 
-    for k in (1, 3):
+    for k in (1, 3, 2):
         half = ((y + k) % 4) // 2
         send(xt_in.at[half], xb.at[c, x, y], y_s.at[k], y_r.at[k], ring_y[k - 1])
-    send(xt_in, ib.at[c, h], y_s.at[2], y_r.at[2], across)
     right_away = remote(right_in, right_slot(zbit), r_s.at[0], r_r.at[0], pair_z)
     pl.when(away)(right_away.start)
 
@@ -122,15 +121,15 @@
         slope = s * (1.0 + pre * (1.0 - s))
         gb[c, h, n] = (gates[2, :, cols].astype(F32) * gates[1, :, cols].astype(F32) * slope).astype(BF16)
         mine = gb.at[c, h, n]
-        send(mine, mine, gy_s.at[p], gy_r.at[p], across)
+        send(mine, relay.at[p], gr_s.at[p], gr_r.at[p], ring_y[2 * (p % 2)])
         send(mine, mine, gc_s.at[p], gc_r.at[p], sibling)
+        if p == 1:
+            send(xt_in.at[h], ib.at[c, h, h], y_s.at[0], y_r.at[0], across)
     loads[0].wait()
     loads[1].wait()
 
-    for k in (1, 3):
+    for k in (1, 3, 2):
         arrive(xb.at[c, x, (y + 4 - k) % 4], y_s.at[k], y_r.at[k])
-    arrive(ib.at[c, 1 - h], y_s.at[2], y_r.at[2])
-    xb[c, x, (y + 2) % 4] = ib[c, 1 - h, h]
 
     def pieces(core, place, k):
         return xb.at[core, place, pl.ds(2 * k, 2)]
@@ -141,13 +140,25 @@
     send(own[1], own[1], x_s.at[2], x_r.at[2], right)
     send(own[0], own[0], x_s.at[3], x_r.at[3], left)
     send(xb.at[c, x], xb.at[c, x], cx_s.at[0], cx_r.at[0], sibling)
-    send(ib.at[c], ib.at[c], cx_s.at[4], cx_r.at[4], sibling)
+    ib[c, 1 - h, h] = xb[c, x, (y + 2) % 4]
+
+    def pass_relay(p):
+        here = relay.at[p]
+        arrive(here, gr_s.at[p], gr_r.at[p])
+        half = ((y + (3 if p % 2 == 0 else 1)) % 4) // 2
+        n = quarter(p, 1 - half if p < 2 else half)
+        send(here, gb.at[c, half, n], gy_s.at[p], gy_r.at[p], ring_y[2 * (p % 2)])
+
+    pass_relay(0)
+    pass_relay(1)
 
     low, high = pieces(c, xl, 0), pieces(c, xr, 1)
     arrive(low, x_s.at[0], x_r.at[0])
     send(low, low, x_s.at[4], x_r.at[4], right)
     arrive(high, x_s.at[1], x_r.at[1])
     send(high, high, x_s.at[5], x_r.at[5], left)
+    pass_relay(2)
+    pass_relay(3)
 
     def pass_gate(p):
         n = quarter(p, h if p < 2 else 1 - h)
@@ -161,6 +172,8 @@
 
     pass_gate(0)
     pass_gate(1)
+    arrive(ib.at[c, 1 - h, 1 - h], y_s.at[0], y_r.at[0])
+    send(ib.at[c], ib.at[c], cx_s.at[4], cx_r.at[4], sibling)
     arrive(ib.at[1 - c], cx_s.at[4], cx_r.at[4])
 
     row = lax.broadcasted_iota(jnp.int32, (256, 160), 0)
@@ -305,9 +318,10 @@
             factors = finish(0)
             for k in range(4):
                 output_ref[:, k * 128:k * 128 + 128] = factors[k * 16:k * 16 + 16]
-            input_ref[:, 0:128] = factors[64:69]
-            input_ref[:, 128:256] = factors[69:74]
-            input_ref[:, 256:320] = factors[74:79, 0:64]
+            for r in range(5):
+                input_ref[r, :, 0:128] = factors[64 + r:65 + r]
+                input_ref[r, :, 128:256] = factors[69 + r:70 + r]
+                input_ref[r, :, 256:320] = factors[74 + r:75 + r, 0:64]
 
     for i in range(2):
         for stream in TILE_STREAMS:
@@ -382,6 +396,17 @@
             copy.wait_send()
 
 
+def store(a_in, b_in, c_in, a_out, b_out, c_out, sems):
+    copies = [
+        pltpu.make_async_copy(src, dst, sems.at[k])
+        for k, (src, dst) in enumerate(((a_in, a_out), (b_in, b_out), (c_in, c_out)))
+    ]
+    for copy in copies:
+        copy.start()
+    for copy in copies:
+        copy.wait()
+
+
 def shards(inputs, gate_values, up_values, hidden_cotangent, owners, left_inverse, right_inverse):
     xt = inputs.T.reshape(2, 160, 256)
     vmem = pl.BlockSpec(memory_space=pltpu.VMEM)
@@ -396,6 +421,7 @@
         pltpu.VMEM((2, 4, 4, 160, 256), BF16),
         pltpu.VMEM((2, 2, 2, 160, 256), BF16),
         pltpu.VMEM((2, 2, 4, 256, 256), BF16),
+        pltpu.VMEM((4, 256, 256), BF16),
         pltpu.VMEM((512, 512), F32),
         pltpu.VMEM((256, 128), F32),
         pltpu.VMEM((4, 160, 256), F32),
@@ -410,13 +436,13 @@
         for rows, lanes in zip(STREAM_ROWS, STREAM_LANES)
     ])
     dma = pltpu.SemaphoreType.DMA
-    for shape in ((8,), (4,), (4,), (6,), (6,), (5,), (5,), (4,), (4,), (8,), (8,), (2,), (2,),
+    for shape in ((8,), (4,), (4,), (6,), (6,), (5,), (5,), (4,), (4,), (4,), (4,), (8,), (8,), (2,), (2,),
                   (len(STREAM_ROWS), 2, 8), (len(STREAM_ROWS), 2, 8), (2,), (2,), (4,), (2, 2), (64,), (64,)):
         scratch.append(dma(shape))
     input_rows, output_rows, pre = pl.pallas_call(
         kernel,
         out_shape=(
-            jax.ShapeDtypeStruct((5, 320), F32),
+            jax.ShapeDtypeStruct((5, 1, 320), F32),
             jax.ShapeDtypeStruct((16, 512), F32),
             jax.ShapeDtypeStruct((5, 8, 1024), F32),
         ),
@@ -430,7 +456,17 @@
     )(
         gate_values, up_values, hidden_cotangent, xt, left_inverse[0, 0], right_inverse[0, 0], owners,
     )
-    return input_rows[None], output_rows[None], pre.transpose(1, 0, 2)
+    results = (input_rows, output_rows, pre)
+    input_rows, output_rows, pre = pl.pallas_call(
+        store,
+        out_shape=tuple(jax.ShapeDtypeStruct(r.shape, F32) for r in results),
+        in_specs=[hbm] * 3,
+        out_specs=(hbm,) * 3,
+        scratch_shapes=[dma((3,))],
+        compiler_params=pltpu.CompilerParams(vmem_limit_bytes=62 * 2**20),
+        name="store",
+    )(*results)
+    return input_rows.transpose(1, 0, 2), output_rows[None], pre.transpose(1, 0, 2)
 
 
 def solution(mesh):

time: 102 us -> 95.1 us (0.932)
  local copies, waits for them, and re-layouts: 4.27 us -> 0 us
  Pallas kernels: 96.6 us -> 94.4 us
    unnamed x3 -> x0, local copies, waits for them, and re-layouts: 4.27 us -> none
    pallas_call x1 -> x2, Pallas kernels: 96.6 us -> 94.4 us  [the longest x1 87.1 us: shards(): pl.pallas_call(kernel, out_shape=(jax.ShapeDtypeStruct((5, 1, 320), F32),...]
where the time goes in v3:
time: 95.1 us; the launch traced here: 95 us
  Pallas kernels  94.4 us (99%)
    pallas_call x1, Pallas kernels, shards(): pl.pallas_call(kernel, out_shape=(jax.ShapeDtypeStruct((5, 1, 320), F32),...  87.1 us
    pallas_call x1, Pallas kernels, shards(): pl.pallas_call(store, out_shape=tuple((jax.ShapeDtypeStruct(r.shape, F32)...  7.32 us

profile of v3, /device:TPU:1, one launch (start us, length us, event | category | flops | bytes accessed | tf_op | source)
XLA Modules:
  0.0 95.0 jit_solution(8100302618153620679)
XLA Ops:
  0.6 87.1 %kfac.1 = (f32[5,1,320]{2,1,0:T(1,128)}, f32[16,512]{1,0:T(8,128)}, f32[5,8,1024]{2,1,0:T(8,128)}) custom-call(bf16[256,1024]{1,0:T(8,128)(2,1)} %gate_in.1, bf16[256,1024]{1,0:T(8,128)(2,1)} %up_in.1, bf16[256,1024]{1,0:T(8,128)(2,1)} %cot_in.1, bf16[2,160,256]{2,1,0:T(8,128)(2,1)} %bitcast.10, f32[320,320]{1,0:T(8,128)} %bitcast.8, f32[512,128]{1,0:T(8,128)} %bitcast.9, ...), custom_call_target="tpu_custom_call" | custom-call | tf_op jit(solution)/shard_map/kfac/pallas_call | solution.py:442
  87.7 7.3 %store.1 = (f32[5,1,320]{2,1,0:T(1,128)}, f32[16,512]{1,0:T(8,128)}, f32[5,8,1024]{2,1,0:T(8,128)}) custom-call(f32[5,1,320]{2,1,0:T(1,128)} %get-tuple-element.9.a_in, f32[16,512]{1,0:T(8,128)} %get-tuple-element.10.b_in, f32[5,8,1024]{2,1,0:T(8,128)} %get-tuple-element.11.c_in), custom_call_target="tpu_custom_call" | custom-call | tf_op jit(solution)/shard_map/store/pallas_call | solution.py:460

commit v4 on v3

--- a/solution.py
+++ b/solution.py
@@ -12,7 +12,7 @@
 REACH = 4
 ORDER = (8, 7, 3, 6, 2, 5, 1, 4)
 TOTAL = 16384
-LEAD = 3
+LEAD = 1
 STREAM_ROWS = (80, 80, 80)
 STREAM_FIRST = (0, 0, 80)
 STREAM_LANES = (128, 256, 256)
@@ -176,6 +176,74 @@
     send(ib.at[c], ib.at[c], cx_s.at[4], cx_r.at[4], sibling)
     arrive(ib.at[1 - c], cx_s.at[4], cx_r.at[4])
 
+    def held_tile(t):
+        slot = (t % 2) * 8 + t // 2
+        held = jnp.int32(0)
+        for k in range(16):
+            held = jnp.maximum(held, jnp.where(owner_ref[0, k] == slot, k, 0))
+        return held
+
+    def partial_tile(t, slot):
+        held = held_tile(t)
+        px, py, pc = held >> 2, (held >> 1) & 1, held & 1
+        total = jnp.zeros((160, 256), F32)
+        for k in range(2):
+            for m in range(2):
+                total += jnp.dot(xb[k, px, 2 * m + py], gb[k, m, 2 * pc + c], preferred_element_type=F32)
+        part[slot] = total
+
+    def factor_rows(t):
+        o_rows = pl.ds(pl.multiple_of(t * 32 + c * 16, 16), 16)
+        i_rows = pl.ds(pl.multiple_of(t * 16, 16), 16)
+        return jnp.concatenate(
+            [osum[o_rows, k * 128:k * 128 + 128] for k in range(4)] + [isum[i_rows, :]], axis=0
+        )
+
+
+    def target(way, distance):
+        return (z + distance) % Z if way == 0 else (z + Z - distance) % Z
+
+    def place(index, way):
+        return 0 if index == 0 else (index % 2) * 2 + way
+
+    def own_part(stream, index, way):
+        if stream == 0:
+            return factor_rows(target(way, ORDER[index] if index < 8 else 0))
+        return part[place(index, way), pl.ds(STREAM_FIRST[stream], STREAM_ROWS[stream])]
+
+    def landed(stream, way, distance):
+        came = ring[stream][0].at[way, distance - 1]
+        arrive(came, rs_s.at[stream, way, distance - 1], rs_r.at[stream, way, distance - 1])
+        return came[...].astype(F32)
+
+    def hop(stream, index):
+        distance = ORDER[index]
+        for way in range(2):
+            farthest = 8 if way == LONG_WAY[stream] else 7
+            if distance > farthest:
+                continue
+            value = own_part(stream, index, way)
+            if distance not in (farthest, REACH - 1):
+                value = value + landed(stream, way, distance + 1)
+            out = ring[stream][1].at[way, distance - 1]
+            out[...] = value.astype(BF16)
+            to = leap_z if distance == REACH else step_z
+            send(out, ring[stream][0].at[way, distance - 1], rs_s.at[stream, way, distance - 1],
+                 rs_r.at[stream, way, distance - 1], to[way])
+
+    def finish(stream):
+        value = own_part(stream, 8, 0)
+        for distance in (1, REACH):
+            for way in range(2):
+                value = value + landed(stream, way, distance)
+        return value * (1.0 / TOTAL)
+
+    arrive(pieces(c, xl, 1), x_s.at[2], x_r.at[2])
+    send(xb.at[c, xl], xb.at[c, xl], cx_s.at[1], cx_r.at[1], sibling)
+    arrive(pieces(c, xr, 0), x_s.at[3], x_r.at[3])
+    send(xb.at[c, xr], xb.at[c, xr], cx_s.at[2], cx_r.at[2], sibling)
+    pass_gate(2)
+    pass_gate(3)
     row = lax.broadcasted_iota(jnp.int32, (256, 160), 0)
     col = lax.broadcasted_iota(jnp.int32, (256, 160), 1)
     start = (row >> 4) * 10 + c * 5
@@ -210,77 +278,7 @@
                     )
             osum[pl.ds(i * 256, 256), pl.ds(j * 256, 256)] = total
 
-    def held_tile(t):
-        slot = (t % 2) * 8 + t // 2
-        held = jnp.int32(0)
-        for k in range(16):
-            held = jnp.maximum(held, jnp.where(owner_ref[0, k] == slot, k, 0))
-        return held
-
-    def partial_tile(t, slot):
-        held = held_tile(t)
-        px, py, pc = held >> 2, (held >> 1) & 1, held & 1
-        total = jnp.zeros((160, 256), F32)
-        for k in range(2):
-            for m in range(2):
-                total += jnp.dot(xb[k, px, 2 * m + py], gb[k, m, 2 * pc + c], preferred_element_type=F32)
-        part[slot] = total
-
-    def factor_rows(t):
-        o_rows = pl.ds(pl.multiple_of(t * 32 + c * 16, 16), 16)
-        i_rows = pl.ds(pl.multiple_of(t * 16, 16), 16)
-        return jnp.concatenate(
-            [osum[o_rows, k * 128:k * 128 + 128] for k in range(4)] + [isum[i_rows, :]], axis=0
-        )
-
-
-    def target(way, distance):
-        return (z + distance) % Z if way == 0 else (z + Z - distance) % Z
-
-    def place(index, way):
-        return 0 if index == 0 else (index % 2) * 2 + way
-
-    def own_part(stream, index, way):
-        if stream == 0:
-            return factor_rows(target(way, ORDER[index] if index < 8 else 0))
-        return part[place(index, way), pl.ds(STREAM_FIRST[stream], STREAM_ROWS[stream])]
-
-    def landed(stream, way, distance):
-        came = ring[stream][0].at[way, distance - 1]
-        arrive(came, rs_s.at[stream, way, distance - 1], rs_r.at[stream, way, distance - 1])
-        return came[...].astype(F32)
-
-    def hop(stream, index):
-        distance = ORDER[index]
-        for way in range(2):
-            farthest = 8 if way == LONG_WAY[stream] else 7
-            if distance > farthest:
-                continue
-            value = own_part(stream, index, way)
-            if distance not in (farthest, REACH - 1):
-                value = value + landed(stream, way, distance + 1)
-            out = ring[stream][1].at[way, distance - 1]
-            out[...] = value.astype(BF16)
-            to = leap_z if distance == REACH else step_z
-            send(out, ring[stream][0].at[way, distance - 1], rs_s.at[stream, way, distance - 1],
-                 rs_r.at[stream, way, distance - 1], to[way])
-
-    def finish(stream):
-        value = own_part(stream, 8, 0)
-        for distance in (1, REACH):
-            for way in range(2):
-                value = value + landed(stream, way, distance)
-        return value * (1.0 / TOTAL)
-
     hop(0, 0)
-    arrive(pieces(c, xl, 1), x_s.at[2], x_r.at[2])
-    send(xb.at[c, xl], xb.at[c, xl], cx_s.at[1], cx_r.at[1], sibling)
-    arrive(pieces(c, xr, 0), x_s.at[3], x_r.at[3])
-    send(xb.at[c, xr], xb.at[c, xr], cx_s.at[2], cx_r.at[2], sibling)
-    hop(0, 1)
-    pass_gate(2)
-    pass_gate(3)
-    hop(0, 2)
     arrive(pieces(c, far, 0), x_s.at[4], x_r.at[4])
     arrive(pieces(c, far, 1), x_s.at[5], x_r.at[5])
     send(xb.at[c, far], xb.at[c, far], cx_s.at[3], cx_r.at[3], sibling)
@@ -315,14 +313,6 @@
         if step == 5:
             pl.when(away)(right_on.wait_recv)
             rsplit[0], rsplit[1] = split(rb[...])
-            factors = finish(0)
-            for k in range(4):
-                output_ref[:, k * 128:k * 128 + 128] = factors[k * 16:k * 16 + 16]
-            for r in range(5):
-                input_ref[r, :, 0:128] = factors[64 + r:65 + r]
-                input_ref[r, :, 128:256] = factors[69 + r:70 + r]
-                input_ref[r, :, 256:320] = factors[74 + r:75 + r, 0:64]
-
     for i in range(2):
         for stream in TILE_STREAMS:
             first = STREAM_FIRST[stream] - i * 80
@@ -330,6 +320,14 @@
                 piece[c, i, pl.ds(first, STREAM_ROWS[stream])] = finish(stream)
         mine = piece.at[c, i]
         send(mine, mine, p_s.at[i], p_r.at[i], sibling)
+    factors = finish(0)
+    for k in range(4):
+        output_ref[:, k * 128:k * 128 + 128] = factors[k * 16:k * 16 + 16]
+    for r in range(5):
+        input_ref[r, :, 0:128] = factors[64 + r:65 + r]
+        input_ref[r, :, 128:256] = factors[69 + r:70 + r]
+        input_ref[r, :, 256:320] = factors[74 + r:75 + r, 0:64]
+
     goes = dev(x, zbit * 2 + ylo, zx, c)
     stay_copies = []
     for i in range(2):
@@ -360,11 +358,20 @@
     def back_copy(to, at):
         return remote(fin.at[pl.ds(to * 5, 5)], ret.at[pl.ds(at * 5, 5)], t_s.at[to], t_r.at[at], (to, tn))
 
+    def holder(off, k):
+        return (k // 2) * 32 + lax.rem(z + off, Z) * 2 + k % 2
+
     def back(i, _):
-        back_copy(lax.rem(dp + i, 64), dp).start()
+        off = 8 + (i + 1) // 2 * (1 - 2 * (i % 2))
+        for k in range(4):
+            back_copy(holder(off, k), dp).start()
         return 0
 
-    lax.fori_loop(1, 64, back, 0)
+    lax.fori_loop(0, 15, back, 0)
+    for k in range(4):
+        @pl.when(holder(0, k) != dp)
+        def _():
+            back_copy(holder(0, k), dp).start()
     ret[pl.ds(dp * 5, 5)] = fin[pl.ds(dp * 5, 5)]
 
     def back_wait(i, _):
@@ -396,14 +403,17 @@
             copy.wait_send()
 
 
-def store(a_in, b_in, c_in, a_out, b_out, c_out, sems):
-    copies = [
-        pltpu.make_async_copy(src, dst, sems.at[k])
-        for k, (src, dst) in enumerate(((a_in, a_out), (b_in, b_out), (c_in, c_out)))
-    ]
-    for copy in copies:
+def store(a_in, b_in, c_in, a_out, b_out, c_out, a_mid, b_mid, c_mid, sems):
+    ways = [(a_in, a_mid, a_out), (b_in, b_mid, b_out)]
+    ways += [(c_in.at[r], c_mid.at[r], c_out.at[r]) for r in range(5)]
+    fetches = [pltpu.make_async_copy(src, mid, sems.at[0, k]) for k, (src, mid, _) in enumerate(ways)]
+    stores = [pltpu.make_async_copy(mid, dst, sems.at[1, k]) for k, (_, mid, dst) in enumerate(ways)]
+    for copy in fetches:
         copy.start()
-    for copy in copies:
+    for fetch, copy in zip(fetches, stores):
+        fetch.wait()
+        copy.start()
+    for copy in stores:
         copy.wait()
 
 
@@ -462,7 +472,7 @@
         out_shape=tuple(jax.ShapeDtypeStruct(r.shape, F32) for r in results),
         in_specs=[hbm] * 3,
         out_specs=(hbm,) * 3,
-        scratch_shapes=[dma((3,))],
+        scratch_shapes=[pltpu.VMEM(r.shape, F32) for r in results] + [dma((2, 7))],
         compiler_params=pltpu.CompilerParams(vmem_limit_bytes=62 * 2**20),
         name="store",
     )(*results)

time: 95.1 us -> 88.7 us (0.933)
  Pallas kernels: 94.4 us -> 87.9 us
    pallas_call x1, Pallas kernels: 7.32 us -> 1.59 us  [shards(): pl.pallas_call(store, out_shape=tuple((jax.ShapeDtypeStruct(r.shape, F32)...]
where the time goes in v4:
time: 88.7 us; the launch traced here: 88.5 us
  Pallas kernels  87.9 us (99%)
    pallas_call x1, Pallas kernels, shards(): pl.pallas_call(kernel, out_shape=(jax.ShapeDtypeStruct((5, 1, 320), F32),...  86.3 us

profile of v4, /device:TPU:1, one launch (start us, length us, event | category | flops | bytes accessed | tf_op | source)
XLA Modules:
  0.0 88.5 jit_solution(6703599996446776588)
XLA Ops:
  0.6 86.3 %kfac.1 = (f32[5,1,320]{2,1,0:T(1,128)}, f32[16,512]{1,0:T(8,128)}, f32[5,8,1024]{2,1,0:T(8,128)}) custom-call(bf16[256,1024]{1,0:T(8,128)(2,1)} %gate_in.1, bf16[256,1024]{1,0:T(8,128)(2,1)} %up_in.1, bf16[256,1024]{1,0:T(8,128)(2,1)} %cot_in.1, bf16[2,160,256]{2,1,0:T(8,128)(2,1)} %bitcast.10, f32[320,320]{1,0:T(8,128)} %bitcast.8, f32[512,128]{1,0:T(8,128)} %bitcast.9, ...), custom_call_target="tpu_custom_call" | custom-call | tf_op jit(solution)/shard_map/kfac/pallas_call | solution.py:452
  86.9 1.6 %store.1 = (f32[5,1,320]{2,1,0:T(1,128)}, f32[16,512]{1,0:T(8,128)}, f32[5,8,1024]{2,1,0:T(8,128)}) custom-call(f32[5,1,320]{2,1,0:T(1,128)} %get-tuple-element.9.a_in, f32[16,512]{1,0:T(8,128)} %get-tuple-element.10.b_in, f32[5,8,1024]{2,1,0:T(8,128)} %get-tuple-element.11.c_in), custom_call_target="tpu_custom_call" | custom-call | tf_op jit(solution)/shard_map/store/pallas_call | solution.py:470

commit v5 on v4

--- a/solution.py
+++ b/solution.py
@@ -10,7 +10,7 @@
 BF16 = jnp.bfloat16
 Z = 16
 REACH = 4
-ORDER = (8, 7, 3, 6, 2, 5, 1, 4)
+ORDER = (8, 7, 6, 3, 5, 2, 4, 1)
 TOTAL = 16384
 LEAD = 1
 STREAM_ROWS = (80, 80, 80)
@@ -320,6 +320,11 @@
                 piece[c, i, pl.ds(first, STREAM_ROWS[stream])] = finish(stream)
         mine = piece.at[c, i]
         send(mine, mine, p_s.at[i], p_r.at[i], sibling)
+    def product(core, i):
+        rows = pl.ds(pl.multiple_of(core * 256, 256), 256)
+        return dot3(split(piece[core, i]), (rsplit[0, rows], rsplit[1, rows]))
+
+    own_products = [product(c, 0), product(c, 1)]
     factors = finish(0)
     for k in range(4):
         output_ref[:, k * 128:k * 128 + 128] = factors[k * 16:k * 16 + 16]
@@ -332,10 +337,7 @@
     stay_copies = []
     for i in range(2):
         arrive(piece.at[1 - c, i], p_s.at[i], p_r.at[i])
-        total = jnp.zeros((80, 256), F32)
-        for k in range(2):
-            rows = slice(k * 256, k * 256 + 256)
-            total += dot3(split(piece[k, i]), (rsplit[0, rows], rsplit[1, rows]))
+        total = own_products[i] + product(1 - c, i)
         rpart[0, i] = total[:, 0:128]
         rpart[1, i] = total[:, 128:256]
         send(rpart.at[1 - zbit, i], worker_part.at[h, i], d_s.at[i], d_r.at[h, i], goes)

time: 88.7 us -> 88.1 us (level)
  no operation moved by 1% of the time
where the time goes in v5:
time: 88.1 us; the launch traced here: 87.9 us
  Pallas kernels  87.2 us (99%)
    pallas_call x1, Pallas kernels, shards(): pl.pallas_call(kernel, out_shape=(jax.ShapeDtypeStruct((5, 1, 320), F32),...  85.6 us

profile of v5, /device:TPU:1, one launch (start us, length us, event | category | flops | bytes accessed | tf_op | source)
XLA Modules:
  0.0 87.9 jit_solution(10750435700478146790)
XLA Ops:
  0.6 85.6 %kfac.1 = (f32[5,1,320]{2,1,0:T(1,128)}, f32[16,512]{1,0:T(8,128)}, f32[5,8,1024]{2,1,0:T(8,128)}) custom-call(bf16[256,1024]{1,0:T(8,128)(2,1)} %gate_in.1, bf16[256,1024]{1,0:T(8,128)(2,1)} %up_in.1, bf16[256,1024]{1,0:T(8,128)(2,1)} %cot_in.1, bf16[2,160,256]{2,1,0:T(8,128)(2,1)} %bitcast.10, f32[320,320]{1,0:T(8,128)} %bitcast.8, f32[512,128]{1,0:T(8,128)} %bitcast.9, ...), custom_call_target="tpu_custom_call" | custom-call | tf_op jit(solution)/shard_map/kfac/pallas_call | solution.py:454
  86.3 1.6 %store.1 = (f32[5,1,320]{2,1,0:T(1,128)}, f32[16,512]{1,0:T(8,128)}, f32[5,8,1024]{2,1,0:T(8,128)}) custom-call(f32[5,1,320]{2,1,0:T(1,128)} %get-tuple-element.9.a_in, f32[16,512]{1,0:T(8,128)} %get-tuple-element.10.b_in, f32[5,8,1024]{2,1,0:T(8,128)} %get-tuple-element.11.c_in), custom_call_target="tpu_custom_call" | custom-call | tf_op jit(solution)/shard_map/store/pallas_call | solution.py:472
